TPU v7x, 32 devices: a whole 2x2x4 slice. The times are simulated.
32 devices in a mesh: grp: 2 (over y), seq: 8 (over z, x), head: 2 (over core).
Axes of the slice: x: 2, y: 2, z: 4, core: 2. Of those that a mesh axis runs over, the one named last changes fastest.
Arguments:
- query_nope: bfloat16 [2048, 8192], P(('grp', 'seq'), 'head'), parts along dimension 0, may hold values from -12 to 12
- query_rope: bfloat16 [2048, 4096], P(('grp', 'seq'), 'head'), parts along dimension 0, may hold values from -400 to 400
- latents: bfloat16 [2048, 576], P(('grp', 'seq')), parts along dimension 0, may hold values from -6 to 6
- key_up: bfloat16 [512, 8192], P('seq', 'head'), may hold values from -0.25 to 0.25
- value_up: bfloat16 [512, 8192], P('seq', 'head'), may hold values from -1 to 1
- query_offset: int32 [16], P(('grp', 'seq')), parts along dimension 0, may hold values from 0 to 2047, as said below
- context_offset: int32 [16], P(('grp', 'seq')), parts along dimension 0, may hold values from 0 to 1920, as said below
Outputs:
- attention: bfloat16 [2048, 8192], P(('grp', 'seq'), 'head'), parts along dimension 0
There are 2 independent parts, one for each index of `grp`. A program takes and returns all parts, laid end to end along the dimension named above; an argument that names none is the same for every part. Nothing has to cross between parts.
Inputs may be any that keep to these rules, and one draw needn't show every extreme that they name: context_offset[s] + 128 <= context_offset[s + 1] for every block s. context_offset[s] <= query_offset[s] < context_offset[s] + 128 for every block s.
All inputs are finite; a program needn't handle non-finite values.
Results may differ from a plain program's by a relative error of at most 0.0068.
Values may be sent and summed in bfloat16 or wider, within the bound.
A program may use at most 64 MiB of HBM per device.

v0:
```python
import math

import jax
import jax.numpy as jnp
from jax import lax
from jax.sharding import PartitionSpec as P

LATENT = 512
ROPE = 64
HEAD_DIM = 128
STEPS = 2


def shifted(x, axis, by):
    peers = lax.axis_size(axis)
    return lax.ppermute(x, axis, [(i, (i + by) % peers) for i in range(peers)])


def fetch_block(latent_block, distance):
    return shifted(latent_block, "seq", distance)


def local(query_nope, query_rope, latents, key_up, value_up, query_offset, context_offset):
    query_rows = query_nope.shape[0]
    kv_rows = latents.shape[0]
    local_heads = key_up.shape[1] // HEAD_DIM
    blocks = [latents]
    for distance in range(STEPS):
        blocks.append(fetch_block(blocks[-1], 1))
    context = jnp.concatenate(blocks, 0)
    latent_cols = context[:, :LATENT]
    rope_keys = context[:, LATENT:]
    key_full, value_full = (
        lax.all_gather(key_up, "seq", axis=0, tiled=True),
        lax.all_gather(value_up, "seq", axis=0, tiled=True),
    )
    key_sums = jnp.dot(latent_cols, key_full, preferred_element_type=jnp.float32)
    value_sums = jnp.dot(latent_cols, value_full, preferred_element_type=jnp.float32)
    key_rows = key_sums.astype(jnp.bfloat16).reshape(-1, local_heads, HEAD_DIM)
    value_rows = value_sums.astype(jnp.bfloat16).reshape(-1, local_heads, HEAD_DIM)
    query_part = query_nope.reshape(query_rows, local_heads, HEAD_DIM)
    rotary_part = query_rope.reshape(query_rows, local_heads, ROPE)
    softmax_scale = 1.0 / math.sqrt(HEAD_DIM + ROPE)
    scores = jnp.einsum("qhd,khd->hqk", query_part, key_rows, preferred_element_type=jnp.float32)
    scores = (
        scores
        + jnp.einsum("qhr,kr->hqk", rotary_part, rope_keys, preferred_element_type=jnp.float32)
    ) * softmax_scale
    query_place = query_offset[0] + jnp.arange(query_rows, dtype=jnp.int32)
    own_place = context_offset[0] + jnp.arange(kv_rows, dtype=jnp.int32)
    mask_list = [own_place[None, :] <= query_place[:, None]]
    for distance in range(STEPS):
        mask_list.append(jnp.ones((query_rows, kv_rows), dtype=bool))
    visible = jnp.concatenate(mask_list, 1)[None, :, :]
    scores = jnp.where(visible, scores, jnp.float32(-1e30))
    highest = jnp.max(scores, axis=2, keepdims=True)
    numerator = jnp.where(visible, jnp.exp(scores - highest), jnp.float32(0.0))
    denominator = jnp.sum(numerator, axis=2, keepdims=True)
    weights_bf = (numerator / denominator).astype(jnp.bfloat16)
    output = jnp.einsum("hqk,khd->qhd", weights_bf, value_rows, preferred_element_type=jnp.float32)
    return output.reshape(query_rows, local_heads * HEAD_DIM).astype(jnp.bfloat16)


def solution(mesh):
    in_specs = (
        P(("grp", "seq"), "head"),
        P(("grp", "seq"), "head"),
        P(("grp", "seq"), None),
        P("seq", "head"),
        P("seq", "head"),
        P(("grp", "seq")),
        P(("grp", "seq")),
    )
    out_specs = P(("grp", "seq"), "head")
    return jax.shard_map(local, mesh=mesh, in_specs=in_specs, out_specs=out_specs, check_vma=False)
```

profile of v0, /device:TPU:0, one launch (start us, length us, event | category | flops | bytes accessed | tf_op | source)
XLA Modules:
  0.0 188.0 jit_solution(4706674367794911595)
XLA Ops:
  6.5 0.0 copy-start
  6.5 0.0 all-gather.3.cloned.1.call-start
  6.5 0.7 all-gather.3.cloned.1.call-update
  7.3 0.0 all-gather.5.cloned.1.call-start
  7.3 0.7 all-gather.5.cloned.1.call-update
  8.0 3.0 %collective-permute-start = (bf16[128,576]{0,1:T(8,128)(2,1)}, bf16[128,576]{0,1:T(8,128)(2,1)S(1)}, u32[]{:S(2)}, u32[]{:S(2)}) collective-permute-start(bf16[128,576]{0,1:T(8,128)(2,1)} %param.9), channel_id=1, source_target_pairs={{0,2},{2,4},{4,6},{6,8},{8,10},{10,12},{12,14},{14,0},{1,3},{3,5},... | collective-permute-start | bytes 442376 | tf_op jit(solution)/shard_map/ppermute | solution.py:16
  12.3 0.1 broadcast_compare_fusion
  12.4 5.7 %collective-permute-done = bf16[128,576]{0,1:T(8,128)(2,1)S(1)} collective-permute-done((bf16[128,576]{0,1:T(8,128)(2,1)}, bf16[128,576]{0,1:T(8,128)(2,1)S(1)}, u32[]{:S(2)}, u32[]{:S(2)}) %collective-permute-start) | collective-permute-done | bytes 147488 | tf_op jit(solution)/shard_map/ppermute | solution.py:16
  18.1 0.0 collective-permute-start.1
  18.1 0.9 constant_dynamic-update-slice_fusion.2
  19.0 1.3 copy.16
  20.5 5.6 %collective-permute-done.1 = bf16[128,576]{0,1:T(8,128)(2,1)S(1)} collective-permute-done((bf16[128,576]{0,1:T(8,128)(2,1)S(1)}, bf16[128,576]{0,1:T(8,128)(2,1)S(1)}, u32[]{:S(2)}, u32[]{:S(2)}) %collective-permute-start.1) | collective-permute-done | bytes 147488 | tf_op jit(solution)/shard_map/ppermute | solution.py:16
  26.1 59.5 %all-gather.3.cloned.1.call-done = bf16[512,4096]{1,0:T(8,128)(2,1)} async-done(((bf16[64,4096]{1,0:T(8,128)(2,1)}), bf16[512,4096]{1,0:T(8,128)(2,1)}) %all-gather.3.cloned.1.call-update) | async-done | bytes 4194320 | tf_op jit(solution)/shard_map/all_gather | solution.py:35
  85.6 5.7 %convolution_convert_fusion.1 = bf16[384,4096]{1,0:T(8,128)(2,1)} fusion(bf16[512,4096]{1,0:T(8,128)(2,1)} %all-gather.3.cloned.1.call-done, bf16[384,576]{0,1:T(8,128)(2,1)S(1)} %constant_dynamic-update-slice_fusion), kind=kOutput, calls=%fused_computation.7 | convolution fusion | flops 1612185600 | bytes 7733248 | tf_op jit(solution)/shard_map/dot_general | solution.py:38
  91.4 4.8 %copy.21 = bf16[384,4096]{0,1:T(8,128)(2,1)} copy(bf16[384,4096]{1,0:T(8,128)(2,1)} %convolution_convert_fusion.1) | data formatting | bytes 6291456 | tf_op jit(solution)/shard_map/reshape | solution.py:40
  96.1 63.3 %all-gather.5.cloned.1.call-done = bf16[512,4096]{1,0:T(8,128)(2,1)} async-done(((bf16[64,4096]{1,0:T(8,128)(2,1)}), bf16[512,4096]{1,0:T(8,128)(2,1)}) %all-gather.5.cloned.1.call-update) | async-done | bytes 4194320 | tf_op jit(solution)/shard_map/all_gather | solution.py:34
  159.4 4.0 %fusion.7 = bf16[48,32,8,128]{3,2,1,0:T(8,128)(2,1)S(1)} fusion(bf16[512,4096]{1,0:T(8,128)(2,1)} %all-gather.5.cloned.1.call-done, bf16[384,576]{0,1:T(8,128)(2,1)S(1)} %constant_dynamic-update-slice_fusion), kind=kOutput, calls=%fused_computation.12 | convolution fusion | flops 1612185600 | bytes 7733248 | tf_op jit(solution)/shard_map/dot_general | solution.py:37
  163.5 0.0 copy-done
  163.5 3.6 %fusion.3 = f32[32,384,128]{2,1,0:T(8,128)} fusion(bf16[48,32,8,128]{3,2,1,0:T(8,128)(2,1)S(1)} %fusion.7, bf16[128,4096]{1,0:T(8,128)(2,1)S(1)} %copy-done), kind=kOutput, calls=%fused_computation.8 | convolution fusion | flops 402653184 | bytes 10485760 | tf_op jit(solution)/shard_map/qhd,khd->hqk/dot_general | solution.py:44
  167.1 8.0 %fusion.13 = (f32[32,128]{1,0:T(8,128)S(1)}, f32[32,128,384]{1,2,0:T(8,128)}) fusion(pred[128,384]{0,1:T(8,128)(4,1)S(1)} %concatenate.8, f32[32,384,128]{2,1,0:T(8,128)} %fusion.3, bf16[128,32,64]{0,2,1:T(8,128)(2,1)S(1)} %bitcast.44, bf16[384,576]{0,1:T(8,128)(2,1)S(1)} %constant_dynamic-update-slice_fusion), kind=kOutput, calls=%fused_computation.25 | convolution fusion | flops 210764160 | bytes 13271040 | tf_op jit(solution)/shard_map/sub | solution.py:57
  175.1 4.7 %fusion.8 = bf16[32,128,128]{2,1,0:T(8,128)(2,1)S(1)} fusion(bf16[384,32,128]{0,2,1:T(8,128)(2,1)} %bitcast.42, f32[32,128,384]{1,2,0:T(8,128)} %get-tuple-element.6, f32[32,128]{1,0:T(8,128)S(1)} %get-tuple-element.5), kind=kOutput, calls=%fused_computation.13 | convolution fusion | flops 406323200 | bytes 10502144 | tf_op jit(solution)/shard_map/hqk,khd->qhd/dot_general | solution.py:60
  179.8 1.3 copy.19
  (4 shorter events, 0.1 us)
Async XLA Ops:
  6.5 156.9 %copy-start = (bf16[128,4096]{1,0:T(8,128)(2,1)S(1)}, bf16[128,4096]{1,0:T(8,128)(2,1)}, u32[]{:S(2)}) copy-start(bf16[128,4096]{1,0:T(8,128)(2,1)} %param.7) | copy-start | bytes 3145732
  6.5 79.1 %all-gather.3.cloned.1.call-start = ((), (), s32[]{:S(2)}) async-start(), calls=%async_computation | async-start | bytes 4718592 | tf_op jit(solution)/shard_map/all_gather | solution.py:35
  7.3 152.2 %all-gather.5.cloned.1.call-start = ((), (), s32[]{:S(2)}) async-start(), calls=%async_computation.1 | async-start | bytes 4718592 | tf_op jit(solution)/shard_map/all_gather | solution.py:34
  8.0 10.1 %collective-permute-start = (bf16[128,576]{0,1:T(8,128)(2,1)}, bf16[128,576]{0,1:T(8,128)(2,1)S(1)}, u32[]{:S(2)}, u32[]{:S(2)}) collective-permute-start(bf16[128,576]{0,1:T(8,128)(2,1)} %param.9), channel_id=1, source_target_pairs={{0,2},{2,4},{4,6},{6,8},{8,10},{10,12},{12,14},{14,0},{1,3},{3,5},... | collective-permute-start | bytes 442376 | tf_op jit(solution)/shard_map/ppermute | solution.py:16
  18.1 8.0 %collective-permute-start.1 = (bf16[128,576]{0,1:T(8,128)(2,1)S(1)}, bf16[128,576]{0,1:T(8,128)(2,1)S(1)}, u32[]{:S(2)}, u32[]{:S(2)}) collective-permute-start(bf16[128,576]{0,1:T(8,128)(2,1)S(1)} %collective-permute-done), channel_id=1, source_target_pairs={{0,2},{2,4},{4,6},{6,8},{8,10},{10,12},{12,14},{14,0},{1,3},{3,5},... | collective-permute-start | bytes 442376 | tf_op jit(solution)/shard_map/ppermute | solution.py:16
Sparse Core Ops, SparseCore 0:
  9.5 76.0 all-gather.2
  87.7 71.6 all-gather.4
where the time goes:
time: 188 us
  waiting for transfers between devices  136 us (72%)
  matrix products  26.1 us (14%)
  between operations  14.8 us (8%)
  local copies, waits for them, and re-layouts  8.45 us (4%)
  starting transfers between devices  3.03 us (2%)
    all_gather x1, waiting for transfers between devices, local(): lax.all_gather(key_up, 'seq', axis=0, tiled=True)  63.3 us
    all_gather x1, waiting for transfers between devices, local(): lax.all_gather(value_up, 'seq', axis=0, tiled=True)  59.5 us
    ppermute x2, waiting for transfers between devices, shifted(): return lax.ppermute(x, axis, [(i, (i + by) % peers) for i in range(peers)])  11.3 us
    sub x1, matrix products, local(): numerator = jnp.where(visible, jnp.exp(scores - highest), jnp.float32(0.0))  8 us
    dot_general x1, matrix products, local(): jnp.dot(latent_cols, value_full, preferred_element_type=jnp.float32)  5.75 us
    reshape x1, local copies, waits for them, and re-layouts, local(): value_sums.astype(jnp.bfloat16).reshape(-1, local_heads, HEAD_DIM)  4.76 us
    dot_general x1, matrix products, local(): jnp.einsum('hqk,khd->qhd', weights_bf, value_rows, preferred_element_type...  4.73 us
    dot_general x1, matrix products, local(): jnp.dot(latent_cols, key_full, preferred_element_type=jnp.float32)  4.02 us
  transfers between devices with their start and end apart: 4, of which 4 were waited for; matrix products, arithmetic and copies ran while one was open for 7% of the time, Pallas kernels for 0%

commit v1 on v0

--- a/solution.py
+++ b/solution.py
@@ -1,14 +1,19 @@
+import functools
 import math
 
 import jax
 import jax.numpy as jnp
 from jax import lax
+from jax.experimental import pallas as pl
+from jax.experimental.pallas import tpu as pltpu
 from jax.sharding import PartitionSpec as P
 
 LATENT = 512
 ROPE = 64
 HEAD_DIM = 128
 STEPS = 2
+CHUNK_HEADS = 4
+MESH = pl.DeviceIdType.MESH
 
 
 def shifted(x, axis, by):
@@ -20,7 +25,7 @@
     return shifted(latent_block, "seq", distance)
 
 
-def local(query_nope, query_rope, latents, key_up, value_up, query_offset, context_offset):
+def local_general(query_nope, query_rope, latents, key_up, value_up, query_offset, context_offset):
     query_rows = query_nope.shape[0]
     kv_rows = latents.shape[0]
     local_heads = key_up.shape[1] // HEAD_DIM
@@ -61,6 +66,319 @@
     return output.reshape(query_rows, local_heads * HEAD_DIM).astype(jnp.bfloat16)
 
 
+def kernel(
+    pairs, chunks, qn, qr, lat, ku, vu, off, out,
+    w, q, r, blocks, offs, context, ropes, o,
+    own_w, own_q, own_r, own_small, own_o,
+    xw_s, xw_r, xq_s, xq_r, xr_s, xr_r, small_s, small_r,
+    right_s, right_r, left_s, left_r, yw_s, yw_r, xo_s, xo_r,
+):
+    g, s, c = lax.axis_index("grp"), lax.axis_index("seq"), lax.axis_index("head")
+    z, x = s // 2, s % 2
+    mate = 2 * z + 1 - x
+    shard = ku.shape[0]
+    width = w.shape[3]
+    rope_width = r.shape[3]
+    half = chunks * width
+    rope_half = chunks * rope_width
+    to_mate = (g, mate, c)
+    to_group = (1 - g, s, c)
+    to_right = (g, 2 * ((z + 1) % pairs) + x, c)
+    to_left = (g, 2 * ((z + pairs - 1) % pairs) + x, c)
+
+    def remote(src, dst, send, recv, device):
+        return pltpu.make_async_remote_copy(
+            src_ref=src, dst_ref=dst, send_sem=send, recv_sem=recv, device_id=device, device_id_type=MESH
+        )
+
+    def cols(h, j):
+        return pl.ds(pl.multiple_of(h * half + j * width, 128), width)
+
+    def rope_cols(h, j):
+        return pl.ds(pl.multiple_of(h * rope_half + j * rope_width, 128), rope_width)
+
+    def rows(first, count):
+        return pl.ds(pl.multiple_of(first, 16), count)
+
+    def own_copies(j):
+        mine = rows(s * shard, shard)
+        return (
+            pltpu.make_async_copy(ku.at[:, cols(x, j)], w.at[0, j, mine, :], own_w.at[0, j]),
+            pltpu.make_async_copy(vu.at[:, cols(x, j)], w.at[1, j, mine, :], own_w.at[1, j]),
+        )
+
+    def own_query(j):
+        return (
+            pltpu.make_async_copy(qn.at[:, cols(x, j)], q.at[x, j], own_q.at[j]),
+            pltpu.make_async_copy(qr.at[:, rope_cols(x, j)], r.at[x, j], own_r.at[j]),
+        )
+
+    def mate_weights(j, src):
+        return remote(
+            src.at[:, cols(1 - x, j)], w.at[g, j, rows(s * shard, shard), :], xw_s.at[j], xw_r.at[j], to_mate
+        )
+
+    def mate_query(j):
+        return (
+            remote(qn.at[:, cols(1 - x, j)], q.at[x, j], xq_s.at[j], xq_r.at[j], to_mate),
+            remote(qr.at[:, rope_cols(1 - x, j)], r.at[x, j], xr_s.at[j], xr_r.at[j], to_mate),
+        )
+
+    def payload(j, place):
+        return w.at[g, j, rows(place * 2 * shard, 2 * shard), :]
+
+    def go_right(j, d):
+        ref = payload(j, z - d + 1)
+        return remote(ref, ref, right_s.at[j, d], right_r.at[j, d], to_right)
+
+    def go_left(j, d):
+        ref = payload(j, z + d - 1)
+        return remote(ref, ref, left_s.at[j, d], left_r.at[j, d], to_left)
+
+    def across_mate(j):
+        ref = w.at[g, j, rows(mate * shard, shard), :]
+        return remote(ref, ref, yw_s.at[j, 0], yw_r.at[j, 0], to_group)
+
+    def across(j, place, slot):
+        ref = payload(j, place)
+        return remote(ref, ref, yw_s.at[j, slot], yw_r.at[j, slot], to_group)
+
+    own_small_copies = (
+        pltpu.make_async_copy(lat, blocks.at[2 + x], own_small.at[0]),
+        pltpu.make_async_copy(off, offs.at[x], own_small.at[1]),
+    )
+    lat_mate = remote(lat, blocks.at[2 + x], small_s.at[0], small_r.at[0], to_mate)
+    off_mate = remote(off, offs.at[x], small_s.at[1], small_r.at[1], to_mate)
+    lat_right = remote(lat, blocks.at[x], small_s.at[2], small_r.at[2], to_right)
+    lat_on = remote(blocks.at[x], blocks.at[x], small_s.at[3], small_r.at[3], to_mate)
+
+    def result_own(j):
+        return pltpu.make_async_copy(o.at[x, j], out.at[:, cols(x, j)], own_o.at[j])
+
+    def result_mate(j):
+        return remote(o.at[1 - x, j], out.at[:, cols(x, j)], xo_s.at[j], xo_r.at[j], to_mate)
+
+    def start_own(j, carry):
+        for copy in own_copies(j):
+            copy.start()
+        return carry
+
+    lax.fori_loop(0, chunks, start_own, 0)
+    for copy in own_small_copies:
+        copy.start()
+
+    barrier = pltpu.get_barrier_semaphore()
+    for device in (to_mate, to_group, to_right, to_left):
+        pl.semaphore_signal(barrier, inc=1, device_id=device, device_id_type=MESH)
+    pl.semaphore_wait(barrier, 4)
+
+    def start_mate(j, carry):
+        @pl.when(g == 0)
+        def _():
+            mate_weights(j, ku).start()
+
+        @pl.when(g != 0)
+        def _():
+            mate_weights(j, vu).start()
+
+        return carry
+
+    lax.fori_loop(0, chunks, start_mate, 0)
+    lat_right.start()
+    lat_mate.start()
+    off_mate.start()
+
+    def enter(j):
+        for copy in own_query(j) + mate_query(j):
+            copy.start()
+        for copy in own_copies(j):
+            copy.wait()
+        mate_weights(j, ku).wait_recv()
+
+        @pl.when(z + 1 < pairs)
+        def _():
+            go_right(j, 1).start()
+
+        @pl.when(z > 0)
+        def _():
+            go_left(j, 1).start()
+
+        across_mate(j).start()
+
+    def hand_on(j, d):
+        @pl.when(z >= d)
+        def _():
+            go_right(j, d).wait_recv()
+
+            @pl.when(z + 1 < pairs)
+            def _():
+                if d + 1 < pairs:
+                    go_right(j, d + 1).start()
+
+            across(j, z - d, d).start()
+
+        @pl.when(z + d < pairs)
+        def _():
+            go_left(j, d).wait_recv()
+
+            @pl.when(z > 0)
+            def _():
+                if d + 1 < pairs:
+                    go_left(j, d + 1).start()
+
+            across(j, z + d, pairs - 1 + d).start()
+
+    def for_arrivals(j, method):
+        getattr(across_mate(j), method)()
+        for d in range(1, pairs):
+            @pl.when(z >= d)
+            def _():
+                getattr(across(j, z - d, d), method)()
+
+            @pl.when(z + d < pairs)
+            def _():
+                getattr(across(j, z + d, pairs - 1 + d), method)()
+
+    def prepare():
+        lat_on.wait_recv()
+        lat_mate.wait_recv()
+        off_mate.wait_recv()
+        for copy in own_small_copies:
+            copy.wait()
+        kv = lat.shape[0]
+        none = jnp.zeros((kv, ROPE), jnp.bfloat16)
+        for k in range(4):
+            context[k * kv:(k + 1) * kv, :] = blocks[k, :, :LATENT]
+            rope_keys = blocks[k, :, LATENT:]
+            ropes[0, k * kv:(k + 1) * kv, :] = jnp.concatenate([rope_keys, none], 1)
+            ropes[1, k * kv:(k + 1) * kv, :] = jnp.concatenate([none, rope_keys], 1)
+
+    def attend(j):
+        for copy in own_query(j):
+            copy.wait()
+        for copy in mate_query(j):
+            copy.wait_recv()
+        kv = lat.shape[0]
+        tokens = qn.shape[0]
+        keys = jnp.dot(context[...], w[0, j], preferred_element_type=jnp.float32).astype(jnp.bfloat16)
+        values = jnp.dot(context[...], w[1, j], preferred_element_type=jnp.float32).astype(jnp.bfloat16)
+        factor = math.log2(math.e) / math.sqrt(HEAD_DIM + ROPE)
+        token = lax.broadcasted_iota(jnp.int32, (tokens, kv), 0)
+        row = lax.broadcasted_iota(jnp.int32, (tokens, kv), 1)
+        for b in range(2):
+            seen = slice(b * kv, (b + 1 + STEPS) * kv)
+            visible = row <= token + offs[b, 0:1, :]
+            for h in range(width // HEAD_DIM):
+                lanes = slice(h * HEAD_DIM, (h + 1) * HEAD_DIM)
+                pair_lanes = slice(h // 2 * 2 * ROPE, (h // 2 + 1) * 2 * ROPE)
+                query = jnp.concatenate([q[b, j, :, lanes], r[b, j, :, pair_lanes]], 1)
+                key = jnp.concatenate([keys[seen, lanes], ropes[h % 2, seen, :]], 1)
+                scores = lax.dot_general(query, key, (((1,), (1,)), ((), ())), preferred_element_type=jnp.float32)
+                scores = jnp.concatenate(
+                    [scores[:, :STEPS * kv], jnp.where(visible, scores[:, STEPS * kv:], jnp.float32(-1e30))], 1
+                )
+                highest = jnp.max(scores, axis=1, keepdims=True)
+                numerator = jnp.exp2((scores - highest) * factor)
+                inverse = 1.0 / jnp.sum(numerator, axis=1, keepdims=True)
+                weights = (numerator * inverse).astype(jnp.bfloat16)
+                summed = jnp.dot(weights, values[seen, lanes], preferred_element_type=jnp.float32)
+                o[b, j, :, lanes] = summed.astype(jnp.bfloat16)
+        result_mate(j).start()
+        result_own(j).start()
+
+    def step(t, carry):
+        @pl.when(t < chunks)
+        def _():
+            enter(t)
+
+        @pl.when(t == 0)
+        def _():
+            lat_right.wait_recv()
+            lat_on.start()
+
+        for d in range(1, pairs):
+            @pl.when((t >= d) & (t < chunks + d))
+            def _():
+                hand_on(t - d, d)
+
+        @pl.when(t == pairs)
+        def _():
+            prepare()
+
+        @pl.when(t >= pairs)
+        def _():
+            for_arrivals(t - pairs, "wait_recv")
+            attend(t - pairs)
+
+        return carry
+
+    lax.fori_loop(0, chunks + pairs, step, 0)
+
+    lat_right.wait_send()
+    lat_mate.wait_send()
+    off_mate.wait_send()
+    lat_on.wait_send()
+
+    def finish(j, carry):
+        mate_weights(j, ku).wait_send()
+        for copy in mate_query(j):
+            copy.wait_send()
+        for d in range(1, pairs):
+            @pl.when((z >= d - 1) & (z + 1 < pairs))
+            def _():
+                go_right(j, d).wait_send()
+
+            @pl.when((z + d - 1 < pairs) & (z > 0))
+            def _():
+                go_left(j, d).wait_send()
+
+        for_arrivals(j, "wait_send")
+        result_own(j).wait()
+        result_mate(j).wait()
+        return carry
+
+    lax.fori_loop(0, chunks, finish, 0)
+
+
+def local_pairs(n_seq, query_nope, query_rope, latents, key_up, value_up, query_offset, context_offset):
+    tokens = query_nope.shape[0]
+    kv = latents.shape[0]
+    heads = key_up.shape[1] // HEAD_DIM
+    pairs = n_seq // 2
+    chunks = heads // 2 // CHUNK_HEADS
+    width = CHUNK_HEADS * HEAD_DIM
+    rope_width = CHUNK_HEADS * ROPE
+    ahead = jnp.broadcast_to((query_offset - context_offset)[:, None], (8, kv))
+    dma = pltpu.SemaphoreType.DMA
+    bf16 = jnp.bfloat16
+    slots = 2 * pairs - 1
+    return pl.pallas_call(
+        functools.partial(kernel, pairs, chunks),
+        out_shape=jax.ShapeDtypeStruct(query_nope.shape, bf16),
+        in_specs=[pl.BlockSpec(memory_space=pl.ANY)] * 6,
+        out_specs=pl.BlockSpec(memory_space=pl.ANY),
+        scratch_shapes=[
+            pltpu.VMEM((2, chunks, LATENT, width), bf16),
+            pltpu.VMEM((2, chunks, tokens, width), bf16),
+            pltpu.VMEM((2, chunks, tokens, rope_width), bf16),
+            pltpu.VMEM((4,) + latents.shape, bf16),
+            pltpu.VMEM((2, 8, kv), jnp.int32),
+            pltpu.VMEM((4 * kv, LATENT), bf16),
+            pltpu.VMEM((2, 4 * kv, 2 * ROPE), bf16),
+            pltpu.VMEM((2, chunks, tokens, width), bf16),
+            dma((2, chunks)), dma((chunks,)), dma((chunks,)), dma((2,)), dma((chunks,)),
+            dma((chunks,)), dma((chunks,)), dma((chunks,)), dma((chunks,)), dma((chunks,)), dma((chunks,)),
+            dma((4,)), dma((4,)),
+            dma((chunks, pairs)), dma((chunks, pairs)), dma((chunks, pairs)), dma((chunks, pairs)),
+            dma((chunks, slots)), dma((chunks, slots)), dma((chunks,)), dma((chunks,)),
+        ],
+        compiler_params=pltpu.CompilerParams(
+            collective_id=0, has_side_effects=True, vmem_limit_bytes=40 * 1024 * 1024
+        ),
+        cost_estimate=pl.CostEstimate(flops=5 * 10 ** 9, bytes_accessed=8 * 10 ** 6, transcendentals=2 * 10 ** 6),
+    )(query_nope, query_rope, latents, key_up, value_up, ahead)
+
+
 def solution(mesh):
     in_specs = (
         P(("grp", "seq"), "head"),
@@ -72,4 +390,9 @@
         P(("grp", "seq")),
     )
     out_specs = P(("grp", "seq"), "head")
+    n_seq = mesh.shape["seq"]
+    if mesh.shape["grp"] == 2 and n_seq % 2 == 0 and n_seq >= 6 and LATENT // n_seq % 16 == 0:
+        local = functools.partial(local_pairs, n_seq)
+    else:
+        local = local_general
     return jax.shard_map(local, mesh=mesh, in_specs=in_specs, out_specs=out_specs, check_vma=False)

time: 188 us -> 70.5 us (0.38)
  waiting for transfers between devices: 136 us -> 0 us
  Pallas kernels: 0 us -> 62.4 us
  matrix products: 26.1 us -> 0 us
  between operations: 14.8 us -> 1.33 us
  starting transfers between devices: 3.03 us -> 0 us
  local copies, waits for them, and re-layouts: 8.45 us -> 6.38 us
    all_gather x2 -> x0, waiting for transfers between devices: 123 us -> none  [the longest x1 63.3 us: local(): lax.all_gather(key_up, 'seq', axis=0, tiled=True)]
    pallas_call x0 -> x1, Pallas kernels: none -> 62.4 us  [local_pairs(): pl.pallas_call(functools.partial(kernel, pairs, chunks), out_shape=jax.Sh...]
    dot_general x4 -> x0, matrix products: 18.1 us -> none  [the longest x1 5.75 us: local(): jnp.dot(latent_cols, value_full, preferred_element_type=jnp.float32)]
    ppermute x2 -> x0, waiting for transfers between devices: 11.3 us -> none  [shifted(): return lax.ppermute(x, axis, [(i, (i + by) % peers) for i in range(peers)])]
    sub x1 -> x0, matrix products: 8 us -> none  [local(): numerator = jnp.where(visible, jnp.exp(scores - highest), jnp.float32(0.0))]
    reshape x1 -> x0, local copies, waits for them, and re-layouts: 4.76 us -> none  [local(): value_sums.astype(jnp.bfloat16).reshape(-1, local_heads, HEAD_DIM)]
    unnamed x5 -> x10, local copies, waits for them, and re-layouts: 2.32 us -> 6.38 us
    ppermute x2 -> x0, starting transfers between devices: 2.99 us -> none  [shifted(): return lax.ppermute(x, axis, [(i, (i + by) % peers) for i in range(peers)])]
  transfers between devices with their start and end apart: 4 -> 0, of which waited for: 4 -> 0; matrix products, arithmetic and copies ran while one was open for 7% -> 0% of each run, Pallas kernels for 0% -> 0%
where the time goes in v1:
time: 70.5 us; the launch traced here: 70.1 us
  Pallas kernels  62.4 us (89%)
  local copies, waits for them, and re-layouts  6.38 us (9%)
  between operations  1.33 us (2%)
    pallas_call x1, Pallas kernels, local_pairs(): pl.pallas_call(functools.partial(kernel, pairs, chunks), out_shape=jax.Sh...  62.4 us
    unnamed x10, local copies, waits for them, and re-layouts  6.38 us

profile of v1, /device:TPU:0, one launch (start us, length us, event | category | flops | bytes accessed | tf_op | source)
XLA Modules:
  0.0 70.1 jit_solution(11254861415037959089)
XLA Ops:
  1.3 1.1 %copy.8.lat = bf16[128,576]{1,0:T(8,128)(2,1)S(1)} copy(bf16[128,576]{0,1:T(8,128)(2,1)} %param.9) | data formatting | bytes 294912 | tf_op args[2]
  2.4 0.0 copy-start
  2.4 1.2 %copy-done = bf16[128,4096]{1,0:T(8,128)(2,1)S(1)} copy-done((bf16[128,4096]{1,0:T(8,128)(2,1)S(1)}, bf16[128,4096]{1,0:T(8,128)(2,1)}, u32[]{:S(2)}) %copy-start) | copy-done | bytes 1048600
  3.6 0.0 copy-start.1
  3.6 1.0 %copy-done.1 = bf16[128,2048]{1,0:T(8,128)(2,1)S(1)} copy-done((bf16[128,2048]{1,0:T(8,128)(2,1)S(1)}, bf16[128,2048]{1,0:T(8,128)(2,1)}, u32[]{:S(2)}) %copy-start.1) | copy-done | bytes 524312
  4.6 0.0 copy-start.2
  4.6 1.0 %copy-done.2 = bf16[64,4096]{1,0:T(8,128)(2,1)S(1)} copy-done((bf16[64,4096]{1,0:T(8,128)(2,1)S(1)}, bf16[64,4096]{1,0:T(8,128)(2,1)}, u32[]{:S(2)}) %copy-start.2) | copy-done | bytes 524312
  5.7 0.0 copy-start.3
  5.7 1.0 %copy-done.3 = bf16[64,4096]{1,0:T(8,128)(2,1)S(1)} copy-done((bf16[64,4096]{1,0:T(8,128)(2,1)S(1)}, bf16[64,4096]{1,0:T(8,128)(2,1)}, u32[]{:S(2)}) %copy-start.3) | copy-done | bytes 524312
  6.7 62.4 %shard_map.73 = bf16[128,4096]{1,0:T(8,128)(2,1)S(1)} custom-call(bf16[128,4096]{1,0:T(8,128)(2,1)S(1)} %copy-done, bf16[128,2048]{1,0:T(8,128)(2,1)S(1)} %copy-done.1, bf16[128,576]{1,0:T(8,128)(2,1)S(1)} %copy.8.lat, bf16[64,4096]{1,0:T(8,128)(2,1)S(1)} %copy-done.2, bf16[64,4096]{1,0:T(8,128)(2,1)S(1)} %copy-done.3, s32[8,128]{1,0:T(8,128)S(1)} %broadcast_in_dim.9.off), custom_call_target="tpu_custom_call" | custom-call | flops 5000000000 | bytes 8000000 | tf_op jit(solution)/shard_map/pallas_call | solution.py:355
  69.2 1.0 %copy.12 = bf16[128,4096]{1,0:T(8,128)(2,1)} copy(bf16[128,4096]{1,0:T(8,128)(2,1)S(1)} %shard_map.73) | data formatting | bytes 2097152
  (1 shorter events, 0.0 us)
Async XLA Ops:
  2.4 1.2 %copy-start = (bf16[128,4096]{1,0:T(8,128)(2,1)S(1)}, bf16[128,4096]{1,0:T(8,128)(2,1)}, u32[]{:S(2)}) copy-start(bf16[128,4096]{1,0:T(8,128)(2,1)} %qn.1) | copy-start | bytes 3145732
  3.6 1.0 %copy-start.1 = (bf16[128,2048]{1,0:T(8,128)(2,1)S(1)}, bf16[128,2048]{1,0:T(8,128)(2,1)}, u32[]{:S(2)}) copy-start(bf16[128,2048]{1,0:T(8,128)(2,1)} %qr.1) | copy-start | bytes 1572868
  4.6 1.0 %copy-start.2 = (bf16[64,4096]{1,0:T(8,128)(2,1)S(1)}, bf16[64,4096]{1,0:T(8,128)(2,1)}, u32[]{:S(2)}) copy-start(bf16[64,4096]{1,0:T(8,128)(2,1)} %ku.1) | copy-start | bytes 1572868
  5.7 1.0 %copy-start.3 = (bf16[64,4096]{1,0:T(8,128)(2,1)S(1)}, bf16[64,4096]{1,0:T(8,128)(2,1)}, u32[]{:S(2)}) copy-start(bf16[64,4096]{1,0:T(8,128)(2,1)} %vu.1) | copy-start | bytes 1572868

commit v2 on v0

--- a/solution.py
+++ b/solution.py
@@ -1,14 +1,20 @@
+import functools
 import math
 
 import jax
 import jax.numpy as jnp
 from jax import lax
+from jax.experimental import pallas as pl
+from jax.experimental.pallas import tpu as pltpu
 from jax.sharding import PartitionSpec as P
 
 LATENT = 512
 ROPE = 64
 HEAD_DIM = 128
 STEPS = 2
+CHUNK_HEADS = 2
+AHEAD = 2
+MESH = pl.DeviceIdType.MESH
 
 
 def shifted(x, axis, by):
@@ -20,7 +26,7 @@
     return shifted(latent_block, "seq", distance)
 
 
-def local(query_nope, query_rope, latents, key_up, value_up, query_offset, context_offset):
+def local_general(query_nope, query_rope, latents, key_up, value_up, query_offset, context_offset):
     query_rows = query_nope.shape[0]
     kv_rows = latents.shape[0]
     local_heads = key_up.shape[1] // HEAD_DIM
@@ -61,6 +67,379 @@
     return output.reshape(query_rows, local_heads * HEAD_DIM).astype(jnp.bfloat16)
 
 
+def kernel(
+    pairs, chunks, q_off, c_off, qn, qr, lat, ku, vu, out,
+    w, q, r, blocks, offs, context, ropes, wide, o,
+    own_w, own_q, own_r, own_lat_sem, own_o,
+    xw_s, xw_r, q_s, q_r, r_s, r_r, lat_s, lat_r, twin_s, twin_r, off_s, off_r,
+    right_s, right_r, left_s, left_r, o_s, o_r,
+):
+    g, s, c = lax.axis_index("grp"), lax.axis_index("seq"), lax.axis_index("head")
+    z, x = s // 2, s % 2
+    me = 2 * g + x
+    mate = 2 * z + 1 - x
+    shard = ku.shape[0]
+    width = q.shape[3]
+    rope_width = r.shape[3]
+    lat_half = lat.shape[0] // 2
+    to_mate = (g, mate, c)
+    to_right = (g, 2 * ((z + 1) % pairs) + x, c)
+    to_left = (g, 2 * ((z + pairs - 1) % pairs) + x, c)
+    to_twin = (g, s, 1 - c)
+
+    def member(k):
+        kg, kx = k // 2, k % 2
+        return g + kg - 2 * g * kg, x + kx - 2 * x * kx
+
+    def to_member(k):
+        mg, mx = member(k)
+        return (mg, 2 * z + mx, c)
+
+    def number(k):
+        mg, mx = member(k)
+        return 2 * mg + mx
+
+    def remote(src, dst, send, recv, device):
+        return pltpu.make_async_remote_copy(
+            src_ref=src, dst_ref=dst, send_sem=send, recv_sem=recv, device_id=device, device_id_type=MESH
+        )
+
+    def cols(quarter, j):
+        return pl.ds(pl.multiple_of((quarter * chunks + j) * width, 128), width)
+
+    def rope_cols(quarter, j):
+        return pl.ds(pl.multiple_of((quarter * chunks + j) * rope_width, 128), rope_width)
+
+    def rows(first, count):
+        return pl.ds(pl.multiple_of(first, 16), count)
+
+    def own_copies(j):
+        mine = rows(s * shard, shard)
+        return [
+            pltpu.make_async_copy(up.at[:, cols(me, j)], w.at[j, mine, m * width:(m + 1) * width], own_w.at[m, j])
+            for m, up in enumerate((ku, vu))
+        ]
+
+    def mate_weights(j):
+        mine = rows(s * shard, shard)
+        quarter = 2 * g + 1 - x
+        return [
+            remote(
+                up.at[:, cols(quarter, j)], w.at[j, mine, m * width:(m + 1) * width], xw_s.at[m, j], xw_r.at[m, j],
+                to_mate,
+            )
+            for m, up in enumerate((ku, vu))
+        ]
+
+    def own_query(j):
+        return [
+            pltpu.make_async_copy(qn.at[:, cols(me, j)], q.at[me, j], own_q.at[j]),
+            pltpu.make_async_copy(qr.at[:, rope_cols(me, j)], r.at[me, j], own_r.at[j]),
+        ]
+
+    def member_query(j):
+        copies = []
+        for k in range(1, 4):
+            copies.append(remote(qn.at[:, cols(number(k), j)], q.at[me, j], q_s.at[k, j], q_r.at[k, j], to_member(k)))
+            copies.append(remote(qr.at[:, rope_cols(number(k), j)], r.at[me, j], r_s.at[k, j], r_r.at[k, j], to_member(k)))
+        return copies
+
+    def payload(j, place):
+        return w.at[j, rows(place * 2 * shard, 2 * shard), :]
+
+    def go_right(j, d, source=None):
+        if source is not None:
+            ref = w.at[j, rows(source * shard, shard), :]
+            slot = pairs * (source % 2)
+            return remote(ref, ref, right_s.at[j, slot], right_r.at[j, slot], to_right)
+        ref = payload(j, z - d + 1)
+        return remote(ref, ref, right_s.at[j, d], right_r.at[j, d], to_right)
+
+    def go_left(j, d, source=None):
+        if source is not None:
+            ref = w.at[j, rows(source * shard, shard), :]
+            slot = pairs * (source % 2)
+            return remote(ref, ref, left_s.at[j, slot], left_r.at[j, slot], to_left)
+        ref = payload(j, z + d - 1)
+        return remote(ref, ref, left_s.at[j, d], left_r.at[j, d], to_left)
+
+    def place(k, current):
+        mg, mx = member(k)
+        return 4 * mg + 2 * current + mx
+
+    def own_part(ref):
+        return ref.at[rows(c * lat_half, lat_half), :]
+
+    own_lat = pltpu.make_async_copy(lat, blocks.at[place(0, 1)], own_lat_sem)
+    lat_right = remote(own_part(lat), own_part(blocks.at[place(0, 0)]), lat_s.at[0, 0], lat_r.at[0, 0], to_right)
+
+    def lat_member(k, current):
+        src = own_part(lat) if current else own_part(blocks.at[place(0, 0)])
+        return remote(src, own_part(blocks.at[place(0, current)]), lat_s.at[k, current], lat_r.at[k, current], to_member(k))
+
+    def lat_twin(k, current):
+        ref = own_part(blocks.at[place(k, current)])
+        return remote(ref, ref, twin_s.at[k, current], twin_r.at[k, current], to_twin)
+
+    def off_member(k):
+        return remote(offs.at[me], offs.at[me], off_s.at[k], off_r.at[k], to_member(k))
+
+    def result_own(j):
+        return pltpu.make_async_copy(o.at[me, j], out.at[:, cols(me, j)], own_o.at[j])
+
+    def result_member(j, k):
+        return remote(o.at[number(k), j], out.at[:, cols(me, j)], o_s.at[k, j], o_r.at[k, j], to_member(k))
+
+    def start_own(j, carry):
+        for copy in own_copies(j):
+            copy.start()
+        return carry
+
+    lax.fori_loop(0, chunks, start_own, 0)
+    own_lat.start()
+    offs[me] = jnp.full(offs.shape[1:], q_off[0] - c_off[0], jnp.int32)
+
+    barrier = pltpu.get_barrier_semaphore()
+    for device in [to_member(k) for k in range(1, 4)] + [to_right, to_left, to_twin]:
+        pl.semaphore_signal(barrier, inc=1, device_id=device, device_id_type=MESH)
+    pl.semaphore_wait(barrier, 6)
+
+    def start_mate(j, carry):
+        for copy in mate_weights(j):
+            copy.start()
+        return carry
+
+    def send(j, source):
+        @pl.when(z + 1 < pairs)
+        def _():
+            go_right(j, 1, source).start()
+
+        @pl.when(z > 0)
+        def _():
+            go_left(j, 1, source).start()
+
+    def enter(j):
+        for copy in own_copies(j):
+            copy.wait()
+        send(j, s)
+        for copy in own_query(j) + member_query(j):
+            copy.start()
+
+    def pass_mate(j):
+        for copy in mate_weights(j):
+            copy.wait_recv()
+        send(j, mate)
+
+    def first(j, carry):
+        enter(j)
+        return carry
+
+    def second(j, carry):
+        pass_mate(j)
+        return carry
+
+    lax.fori_loop(0, chunks, start_mate, 0)
+    lat_right.start()
+    for k in range(1, 4):
+        lat_member(k, 1).start()
+        off_member(k).start()
+    lax.fori_loop(0, AHEAD, first, 0)
+    lax.fori_loop(0, AHEAD, second, 0)
+
+    def hand_on(j, d):
+        @pl.when(z >= d)
+        def _():
+            if d == 1:
+                go_right(j, d, s).wait_recv()
+                go_right(j, d, mate).wait_recv()
+            else:
+                go_right(j, d).wait_recv()
+
+            @pl.when(z + 1 < pairs)
+            def _():
+                if d + 1 < pairs:
+                    go_right(j, d + 1).start()
+
+        @pl.when(z + d < pairs)
+        def _():
+            if d == 1:
+                go_left(j, d, s).wait_recv()
+                go_left(j, d, mate).wait_recv()
+            else:
+                go_left(j, d).wait_recv()
+
+            @pl.when(z > 0)
+            def _():
+                if d + 1 < pairs:
+                    go_left(j, d + 1).start()
+
+    def spread_previous():
+        lat_right.wait_recv()
+        for k in range(1, 4):
+            lat_member(k, 0).start()
+        lat_twin(0, 0).start()
+
+    def spread_twin():
+        for k in range(1, 4):
+            for current in (1, 0):
+                lat_member(k, current).wait_recv()
+                lat_twin(k, current).start()
+
+    def prepare():
+        own_lat.wait()
+        lat_twin(0, 0).wait_recv()
+        for k in range(1, 4):
+            off_member(k).wait_recv()
+            for current in (1, 0):
+                lat_twin(k, current).wait_recv()
+        kv = lat.shape[1]
+        none = jnp.zeros((kv, ROPE), jnp.bfloat16)
+        for k in range(8):
+            context[k * kv:(k + 1) * kv, :] = blocks[k, :LATENT, :].T
+            rope_keys = blocks[k, LATENT:, :].T
+            ropes[0, k * kv:(k + 1) * kv, :] = jnp.concatenate([rope_keys, none], 1)
+            ropes[1, k * kv:(k + 1) * kv, :] = jnp.concatenate([none, rope_keys], 1)
+        wide[:, :, HEAD_DIM:] = jnp.ones((wide.shape[0], 8 * kv, HEAD_DIM), jnp.bfloat16)
+
+    def attend(j):
+        for copy in own_query(j):
+            copy.wait()
+        for copy in member_query(j):
+            copy.wait_recv()
+        kv = lat.shape[1]
+        tokens = qn.shape[0]
+        both = jnp.dot(context[...], w[j], preferred_element_type=jnp.float32).astype(jnp.bfloat16)
+        for h in range(width // HEAD_DIM):
+            wide[h, :, :HEAD_DIM] = both[:, width + h * HEAD_DIM:width + (h + 1) * HEAD_DIM]
+        factor = math.log2(math.e) / math.sqrt(HEAD_DIM + ROPE)
+        token = lax.broadcasted_iota(jnp.int32, (tokens, kv), 0)
+        row = lax.broadcasted_iota(jnp.int32, (tokens, kv), 1)
+        for b in range(4):
+            start = (4 * (b // 2) + b % 2) * kv
+            seen = slice(start, start + (1 + STEPS) * kv)
+            visible = row <= token + offs[b, 0:1, :]
+            for h in range(width // HEAD_DIM):
+                lanes = slice(h * HEAD_DIM, (h + 1) * HEAD_DIM)
+                pair_lanes = slice(h // 2 * 2 * ROPE, (h // 2 + 1) * 2 * ROPE)
+                query = jnp.concatenate([q[b, j, :, lanes], r[b, j, :, pair_lanes]], 1)
+                key = jnp.concatenate([both[seen, lanes], ropes[h % 2, seen, :]], 1)
+                scores = lax.dot_general(query, key, (((1,), (1,)), ((), ())), preferred_element_type=jnp.float32)
+                scores = jnp.concatenate(
+                    [scores[:, :STEPS * kv], jnp.where(visible, scores[:, STEPS * kv:], jnp.float32(-1e30))], 1
+                )
+                highest = jnp.max(scores, axis=1, keepdims=True)
+                numerator = jnp.exp2((scores - highest) * factor).astype(jnp.bfloat16)
+                summed = jnp.dot(numerator, wide[h, seen, :], preferred_element_type=jnp.float32)
+                o[b, j, :, lanes] = (summed[:, :HEAD_DIM] / summed[:, HEAD_DIM:]).astype(jnp.bfloat16)
+        for k in range(3, 0, -1):
+            result_member(j, k).start()
+        result_own(j).start()
+
+    def step(t, carry):
+        @pl.when(t + AHEAD < chunks)
+        def _():
+            enter(t + AHEAD)
+            pass_mate(t + AHEAD)
+
+        @pl.when(t == 0)
+        def _():
+            spread_previous()
+
+        for d in range(1, pairs):
+            @pl.when((t >= d) & (t < chunks + d))
+            def _():
+                hand_on(t - d, d)
+
+        @pl.when(t == 1)
+        def _():
+            spread_twin()
+
+        @pl.when(t == pairs - 1)
+        def _():
+            prepare()
+
+        @pl.when(t >= pairs - 1)
+        def _():
+            attend(t - pairs + 1)
+
+        return carry
+
+    lax.fori_loop(0, chunks + pairs - 1, step, 0)
+
+    lat_right.wait_send()
+    lat_twin(0, 0).wait_send()
+    for k in range(1, 4):
+        off_member(k).wait_send()
+        for current in (1, 0):
+            lat_member(k, current).wait_send()
+            lat_twin(k, current).wait_send()
+
+    def finish(j, carry):
+        for copy in mate_weights(j) + member_query(j):
+            copy.wait_send()
+        for d in range(1, pairs):
+            @pl.when((z >= d - 1) & (z + 1 < pairs))
+            def _():
+                if d == 1:
+                    go_right(j, d, s).wait_send()
+                    go_right(j, d, mate).wait_send()
+                else:
+                    go_right(j, d).wait_send()
+
+            @pl.when((z + d - 1 < pairs) & (z > 0))
+            def _():
+                if d == 1:
+                    go_left(j, d, s).wait_send()
+                    go_left(j, d, mate).wait_send()
+                else:
+                    go_left(j, d).wait_send()
+
+        result_own(j).wait()
+        for k in range(1, 4):
+            result_member(j, k).wait()
+        return carry
+
+    lax.fori_loop(0, chunks, finish, 0)
+
+
+def local_quads(n_seq, query_nope, query_rope, latents, key_up, value_up, query_offset, context_offset):
+    tokens = query_nope.shape[0]
+    kv = latents.shape[0]
+    heads = key_up.shape[1] // HEAD_DIM
+    pairs = n_seq // 2
+    chunks = heads // 4 // CHUNK_HEADS
+    width = CHUNK_HEADS * HEAD_DIM
+    rope_width = CHUNK_HEADS * ROPE
+    dma = pltpu.SemaphoreType.DMA
+    bf16 = jnp.bfloat16
+    return pl.pallas_call(
+        functools.partial(kernel, pairs, chunks),
+        out_shape=jax.ShapeDtypeStruct(query_nope.shape, bf16),
+        in_specs=[pl.BlockSpec(memory_space=pltpu.SMEM)] * 2 + [pl.BlockSpec(memory_space=pltpu.HBM)] * 5,
+        out_specs=pl.BlockSpec(memory_space=pl.ANY),
+        scratch_shapes=[
+            pltpu.VMEM((chunks, LATENT, 2 * width), bf16),
+            pltpu.VMEM((4, chunks, tokens, width), bf16),
+            pltpu.VMEM((4, chunks, tokens, rope_width), bf16),
+            pltpu.VMEM((8, latents.shape[1], kv), bf16),
+            pltpu.VMEM((4, 8, kv), jnp.int32),
+            pltpu.VMEM((8 * kv, LATENT), bf16),
+            pltpu.VMEM((2, 8 * kv, 2 * ROPE), bf16),
+            pltpu.VMEM((CHUNK_HEADS, 8 * kv, 2 * HEAD_DIM), bf16),
+            pltpu.VMEM((4, chunks, tokens, width), bf16),
+            dma((2, chunks)), dma((chunks,)), dma((chunks,)), dma, dma((chunks,)),
+            dma((2, chunks)), dma((2, chunks)), dma((4, chunks)), dma((4, chunks)), dma((4, chunks)), dma((4, chunks)),
+            dma((4, 2)), dma((4, 2)), dma((4, 2)), dma((4, 2)), dma((4,)), dma((4,)),
+            dma((chunks, pairs + 1)), dma((chunks, pairs + 1)), dma((chunks, pairs + 1)), dma((chunks, pairs + 1)),
+            dma((4, chunks)), dma((4, chunks)),
+        ],
+        compiler_params=pltpu.CompilerParams(
+            collective_id=0, has_side_effects=True, vmem_limit_bytes=62 * 1024 * 1024
+        ),
+        cost_estimate=pl.CostEstimate(flops=5 * 10 ** 9, bytes_accessed=8 * 10 ** 6, transcendentals=2 * 10 ** 6),
+    )(query_offset, context_offset, query_nope, query_rope, latents.T, key_up, value_up)
+
+
 def solution(mesh):
     in_specs = (
         P(("grp", "seq"), "head"),
@@ -72,4 +451,9 @@
         P(("grp", "seq")),
     )
     out_specs = P(("grp", "seq"), "head")
+    n_seq = mesh.shape["seq"]
+    if mesh.shape["grp"] == 2 and n_seq % 2 == 0 and n_seq >= 6 and LATENT // n_seq % 16 == 0:
+        local = functools.partial(local_quads, n_seq)
+    else:
+        local = local_general
     return jax.shard_map(local, mesh=mesh, in_specs=in_specs, out_specs=out_specs, check_vma=False)

time: 188 us -> 66.2 us (0.35)
  waiting for transfers between devices: 136 us -> 0 us
  Pallas kernels: 0 us -> 62.5 us
  matrix products: 26.1 us -> 0 us
  between operations: 14.8 us -> 1.3 us
  local copies, waits for them, and re-layouts: 8.45 us -> 2.29 us
  starting transfers between devices: 3.03 us -> 0 us
    all_gather x2 -> x0, waiting for transfers between devices: 123 us -> none  [the longest x1 63.3 us: local(): lax.all_gather(key_up, 'seq', axis=0, tiled=True)]
    pallas_call x0 -> x1, Pallas kernels: none -> 62.5 us  [local_quads(): pl.pallas_call(functools.partial(kernel, pairs, chunks), out_shape=jax.Sh...]
    dot_general x4 -> x0, matrix products: 18.1 us -> none  [the longest x1 5.75 us: local(): jnp.dot(latent_cols, value_full, preferred_element_type=jnp.float32)]
    ppermute x2 -> x0, waiting for transfers between devices: 11.3 us -> none  [shifted(): return lax.ppermute(x, axis, [(i, (i + by) % peers) for i in range(peers)])]
    sub x1 -> x0, matrix products: 8 us -> none  [local(): numerator = jnp.where(visible, jnp.exp(scores - highest), jnp.float32(0.0))]
    reshape x1 -> x0, local copies, waits for them, and re-layouts: 4.76 us -> none  [local(): value_sums.astype(jnp.bfloat16).reshape(-1, local_heads, HEAD_DIM)]
    ppermute x2 -> x0, starting transfers between devices: 2.99 us -> none  [shifted(): return lax.ppermute(x, axis, [(i, (i + by) % peers) for i in range(peers)])]
  transfers between devices with their start and end apart: 4 -> 0, of which waited for: 4 -> 0; matrix products, arithmetic and copies ran while one was open for 7% -> 0% of each run, Pallas kernels for 0% -> 0%
where the time goes in v2:
time: 66.2 us; the launch traced here: 66.1 us
  Pallas kernels  62.5 us (94%)
  local copies, waits for them, and re-layouts  2.29 us (3%)
  between operations  1.3 us (2%)
    pallas_call x1, Pallas kernels, local_quads(): pl.pallas_call(functools.partial(kernel, pairs, chunks), out_shape=jax.Sh...  62.5 us
    unnamed x1, local copies, waits for them, and re-layouts  2.29 us

profile of v2, /device:TPU:0, one launch (start us, length us, event | category | flops | bytes accessed | tf_op | source)
XLA Modules:
  0.0 66.1 jit_solution(11581337434903904293)
XLA Ops:
  1.3 62.5 %shard_map.73 = bf16[128,4096]{1,0:T(8,128)(2,1)} custom-call(s32[1]{0:T(128)S(6)} %copy.9.q_off, s32[1]{0:T(128)S(6)} %copy.10.c_off, bf16[128,4096]{1,0:T(8,128)(2,1)} %qn.1, bf16[128,2048]{1,0:T(8,128)(2,1)} %qr.1, bf16[576,128]{1,0:T(8,128)(2,1)} %bitcast.1, bf16[64,4096]{1,0:T(8,128)(2,1)} %ku.1, bf16[64,4096]{1,0:T(8,128)(2,1)} %vu.1), custom_call_target="tpu_custom_call" | custom-call | flops 5000000000 | bytes 8000000 | tf_op jit(solution)/shard_map/pallas_call | solution.py:415
  63.8 2.3 %copy.11 = bf16[128,4096]{1,0:T(8,128)(2,1)} copy(bf16[128,4096]{1,0:T(8,128)(2,1)} %shard_map.73) | data formatting | bytes 2097152

commit v3 on v2

--- a/solution.py
+++ b/solution.py
@@ -222,14 +222,17 @@
         for copy in own_copies(j):
             copy.wait()
         send(j, s)
-        for copy in own_query(j) + member_query(j):
-            copy.start()
 
     def pass_mate(j):
         for copy in mate_weights(j):
             copy.wait_recv()
         send(j, mate)
 
+    def ask(j, carry):
+        for copy in own_query(j) + member_query(j):
+            copy.start()
+        return carry
+
     def first(j, carry):
         enter(j)
         return carry
@@ -238,13 +241,21 @@
         pass_mate(j)
         return carry
 
-    lax.fori_loop(0, chunks, start_mate, 0)
     lat_right.start()
-    for k in range(1, 4):
+    for k in range(3, 0, -1):
         lat_member(k, 1).start()
         off_member(k).start()
+    lax.fori_loop(0, chunks, start_mate, 0)
     lax.fori_loop(0, AHEAD, first, 0)
+    def spread_previous():
+        lat_right.wait_recv()
+        for k in range(1, 4):
+            lat_member(k, 0).start()
+        lat_twin(0, 0).start()
+
     lax.fori_loop(0, AHEAD, second, 0)
+    spread_previous()
+    lax.fori_loop(0, 1, ask, 0)
 
     def hand_on(j, d):
         @pl.when(z >= d)
@@ -272,12 +283,6 @@
             def _():
                 if d + 1 < pairs:
                     go_left(j, d + 1).start()
-
-    def spread_previous():
-        lat_right.wait_recv()
-        for k in range(1, 4):
-            lat_member(k, 0).start()
-        lat_twin(0, 0).start()
 
     def spread_twin():
         for k in range(1, 4):
@@ -314,23 +319,37 @@
         factor = math.log2(math.e) / math.sqrt(HEAD_DIM + ROPE)
         token = lax.broadcasted_iota(jnp.int32, (tokens, kv), 0)
         row = lax.broadcasted_iota(jnp.int32, (tokens, kv), 1)
-        for b in range(4):
+        pieces = [(b, h) for b in range(4) for h in range(width // HEAD_DIM)]
+
+        def seen(b):
             start = (4 * (b // 2) + b % 2) * kv
-            seen = slice(start, start + (1 + STEPS) * kv)
+            return slice(start, start + (1 + STEPS) * kv)
+
+        def lanes(h):
+            return slice(h * HEAD_DIM, (h + 1) * HEAD_DIM)
+
+        scored = []
+        for b, h in pieces:
+            pair_lanes = slice(h // 2 * 2 * ROPE, (h // 2 + 1) * 2 * ROPE)
+            query = jnp.concatenate([q[b, j, :, lanes(h)], r[b, j, :, pair_lanes]], 1)
+            key = jnp.concatenate([both[seen(b), lanes(h)], ropes[h % 2, seen(b), :]], 1)
+            scored.append(
+                lax.dot_general(query, key, (((1,), (1,)), ((), ())), preferred_element_type=jnp.float32)
+            )
+        numerators = []
+        for (b, h), scores in zip(pieces, scored):
             visible = row <= token + offs[b, 0:1, :]
-            for h in range(width // HEAD_DIM):
-                lanes = slice(h * HEAD_DIM, (h + 1) * HEAD_DIM)
-                pair_lanes = slice(h // 2 * 2 * ROPE, (h // 2 + 1) * 2 * ROPE)
-                query = jnp.concatenate([q[b, j, :, lanes], r[b, j, :, pair_lanes]], 1)
-                key = jnp.concatenate([both[seen, lanes], ropes[h % 2, seen, :]], 1)
-                scores = lax.dot_general(query, key, (((1,), (1,)), ((), ())), preferred_element_type=jnp.float32)
-                scores = jnp.concatenate(
-                    [scores[:, :STEPS * kv], jnp.where(visible, scores[:, STEPS * kv:], jnp.float32(-1e30))], 1
-                )
-                highest = jnp.max(scores, axis=1, keepdims=True)
-                numerator = jnp.exp2((scores - highest) * factor).astype(jnp.bfloat16)
-                summed = jnp.dot(numerator, wide[h, seen, :], preferred_element_type=jnp.float32)
-                o[b, j, :, lanes] = (summed[:, :HEAD_DIM] / summed[:, HEAD_DIM:]).astype(jnp.bfloat16)
+            scores = jnp.concatenate(
+                [scores[:, :STEPS * kv], jnp.where(visible, scores[:, STEPS * kv:], jnp.float32(-1e30))], 1
+            )
+            highest = jnp.max(scores, axis=1, keepdims=True)
+            numerators.append(jnp.exp2((scores - highest) * factor).astype(jnp.bfloat16))
+        sums = [
+            jnp.dot(numerator, wide[h, seen(b), :], preferred_element_type=jnp.float32)
+            for (b, h), numerator in zip(pieces, numerators)
+        ]
+        for (b, h), summed in zip(pieces, sums):
+            o[b, j, :, lanes(h)] = (summed[:, :HEAD_DIM] / summed[:, HEAD_DIM:]).astype(jnp.bfloat16)
         for k in range(3, 0, -1):
             result_member(j, k).start()
         result_own(j).start()
@@ -341,9 +360,9 @@
             enter(t + AHEAD)
             pass_mate(t + AHEAD)
 
-        @pl.when(t == 0)
-        def _():
-            spread_previous()
+        @pl.when(t + 1 < chunks)
+        def _():
+            ask(t + 1, 0)
 
         for d in range(1, pairs):
             @pl.when((t >= d) & (t < chunks + d))

time: 66.2 us -> 55.2 us (0.83)
  Pallas kernels: 62.5 us -> 51.4 us
    pallas_call x1, Pallas kernels: 62.5 us -> 51.4 us  [local_quads(): pl.pallas_call(functools.partial(kernel, pairs, chunks), out_shape=jax.Sh...]
where the time goes in v3:
time: 55.2 us; the launch traced here: 55 us
  Pallas kernels  51.4 us (93%)
  local copies, waits for them, and re-layouts  2.29 us (4%)
  between operations  1.3 us (2%)
    pallas_call x1, Pallas kernels, local_quads(): pl.pallas_call(functools.partial(kernel, pairs, chunks), out_shape=jax.Sh...  51.4 us
    unnamed x1, local copies, waits for them, and re-layouts  2.29 us

profile of v3, /device:TPU:0, one launch (start us, length us, event | category | flops | bytes accessed | tf_op | source)
XLA Modules:
  0.0 55.0 jit_solution(4636433791199902542)
XLA Ops:
  1.3 51.4 %shard_map.73 = bf16[128,4096]{1,0:T(8,128)(2,1)} custom-call(s32[1]{0:T(128)S(6)} %copy.9.q_off, s32[1]{0:T(128)S(6)} %copy.10.c_off, bf16[128,4096]{1,0:T(8,128)(2,1)} %qn.1, bf16[128,2048]{1,0:T(8,128)(2,1)} %qr.1, bf16[576,128]{1,0:T(8,128)(2,1)} %bitcast.1, bf16[64,4096]{1,0:T(8,128)(2,1)} %ku.1, bf16[64,4096]{1,0:T(8,128)(2,1)} %vu.1), custom_call_target="tpu_custom_call" | custom-call | flops 5000000000 | bytes 8000000 | tf_op jit(solution)/shard_map/pallas_call | solution.py:434
  52.7 2.3 %copy.11 = bf16[128,4096]{1,0:T(8,128)(2,1)} copy(bf16[128,4096]{1,0:T(8,128)(2,1)} %shard_map.73) | data formatting | bytes 2097152

commit v4 on v3

--- a/solution.py
+++ b/solution.py
@@ -242,11 +242,11 @@
         return carry
 
     lat_right.start()
+    lax.fori_loop(0, AHEAD, first, 0)
+    lax.fori_loop(0, chunks, start_mate, 0)
     for k in range(3, 0, -1):
         lat_member(k, 1).start()
         off_member(k).start()
-    lax.fori_loop(0, chunks, start_mate, 0)
-    lax.fori_loop(0, AHEAD, first, 0)
     def spread_previous():
         lat_right.wait_recv()
         for k in range(1, 4):

time: 55.2 us -> 53.9 us (0.976)
  Pallas kernels: 51.4 us -> 50.1 us
    pallas_call x1, Pallas kernels: 51.4 us -> 50.1 us  [local_quads(): pl.pallas_call(functools.partial(kernel, pairs, chunks), out_shape=jax.Sh...]
where the time goes in v4:
time: 53.9 us; the launch traced here: 53.7 us
  Pallas kernels  50.1 us (93%)
  local copies, waits for them, and re-layouts  2.29 us (4%)
  between operations  1.3 us (2%)
    pallas_call x1, Pallas kernels, local_quads(): pl.pallas_call(functools.partial(kernel, pairs, chunks), out_shape=jax.Sh...  50.1 us
    unnamed x1, local copies, waits for them, and re-layouts  2.29 us

profile of v4, /device:TPU:0, one launch (start us, length us, event | category | flops | bytes accessed | tf_op | source)
XLA Modules:
  0.0 53.7 jit_solution(18009794780355312109)
XLA Ops:
  1.3 50.1 %shard_map.73 = bf16[128,4096]{1,0:T(8,128)(2,1)} custom-call(s32[1]{0:T(128)S(6)} %copy.9.q_off, s32[1]{0:T(128)S(6)} %copy.10.c_off, bf16[128,4096]{1,0:T(8,128)(2,1)} %qn.1, bf16[128,2048]{1,0:T(8,128)(2,1)} %qr.1, bf16[576,128]{1,0:T(8,128)(2,1)} %bitcast.1, bf16[64,4096]{1,0:T(8,128)(2,1)} %ku.1, bf16[64,4096]{1,0:T(8,128)(2,1)} %vu.1), custom_call_target="tpu_custom_call" | custom-call | flops 5000000000 | bytes 8000000 | tf_op jit(solution)/shard_map/pallas_call | solution.py:434
  51.4 2.3 %copy.11 = bf16[128,4096]{1,0:T(8,128)(2,1)} copy(bf16[128,4096]{1,0:T(8,128)(2,1)} %shard_map.73) | data formatting | bytes 2097152
